TPU v7x, 1024 devices: a whole 4x8x16 slice. The times are simulated.
1024 devices in a mesh: expert: 32 (over x_hi, y, core), dp: 32 (over x_lo, z).
Axes of the slice: x: 4 (x_hi: 2, x_lo: 2; x = x_hi * 2 + x_lo), y: 8, z: 16, core: 2. Of those that a mesh axis runs over, the one named last changes fastest.
Arguments:
- tokens: bfloat16 [6144, 4096], P('expert', 'dp'), may hold values from -6 to 6
- out_grad: bfloat16 [6144, 4096], P('expert', 'dp'), may hold values from -6 to 6
- routes: int32 [6144, 8], P('expert'), may hold values from 0 to 127, all different within a row; in each aligned block of 192 rows (0 to 191, 192 to 383, ...) at most 24 rows name the same one
- scores: float32 [6144, 8], P('expert'), may hold values from 0.05 to 1
- w_gate_up: bfloat16 [32, 4096, 2, 768], P('expert', 'dp'), may hold values from -0.09375 to 0.09375
- w_down: bfloat16 [32, 768, 4096], P('expert', None, 'dp'), may hold values from -0.21875 to 0.21875
Outputs:
- layer_out: bfloat16 [6144, 4096], P('expert', 'dp')
- grad_tokens: bfloat16 [6144, 4096], P('expert', 'dp')
- grad_gate_up: bfloat16 [32, 4096, 2, 768], P('expert', 'dp')
- grad_down: bfloat16 [32, 768, 4096], P('expert', None, 'dp')
Inputs may be any that keep to these rules, and one draw needn't show every extreme that they name: `routes`: in each aligned block of 192 rows (the rows of one index of expert) no id is named by more than 24 rows, a bound that some block reaches.
All inputs are finite; a program needn't handle non-finite values.
Results may differ from a plain program's by a relative error of at most 0.0065.
Values may be sent and summed in bfloat16 or wider, within the bound.
A program may use at most 64 MiB of HBM per device.

v0:
```python
import jax
import jax.numpy as jnp
from jax import lax
from jax.sharding import PartitionSpec as P

CAP = 24


def reduce_width(partial_value):
    return lax.psum_scatter(partial_value, "dp", scatter_dimension=0, tiled=True)


def spread_back(share):
    return lax.all_gather(share, "dp", axis=0, tiled=True)


def forward_share(pre):
    gate = pre[:, 0, :]
    upper = pre[:, 1, :]
    sig = jax.nn.sigmoid(gate)
    act = gate * sig
    return (gate, upper, sig, act, (act * upper).astype(jnp.bfloat16)[:, None, :])


def backward_share(grad_hidden, gate, upper, sig, act):
    grad_gate = grad_hidden * upper * sig * (1.0 + gate * (1.0 - sig))
    grad_upper = grad_hidden * act
    return jnp.stack([grad_gate, grad_upper], axis=1).astype(jnp.bfloat16)


def body(tokens, out_grad, routes, scores, w_gate_up, w_down):
    experts = lax.axis_size("expert")
    tok_rows, width = tokens.shape
    top = routes.shape[1]
    slots = experts * CAP
    combine = scores / jnp.sum(scores, axis=1, keepdims=True)
    kept = routes < experts
    onehot = (routes[:, :, None] == jnp.arange(experts, dtype=jnp.int32)[None, None, :]).astype(
        jnp.int32
    )
    flat_hot = onehot.reshape(tok_rows * top, experts)
    before = jnp.cumsum(flat_hot, axis=0) - flat_hot
    rank = jnp.sum(before * flat_hot, axis=1).reshape(tok_rows, top)
    target = jnp.where(kept, routes * CAP + rank, -1)
    match = target[None, :, :] == jnp.arange(slots, dtype=jnp.int32)[:, None, None]
    place = jnp.sum(match.astype(jnp.float32), axis=2).astype(jnp.bfloat16)
    slot_weight = jnp.sum(jnp.where(match, combine[None, :, :], jnp.float32(0.0)), axis=(1, 2))
    send_rows = jnp.dot(place, tokens, preferred_element_type=jnp.float32).astype(jnp.bfloat16)
    picked_grad = jnp.dot(place, out_grad, preferred_element_type=jnp.float32)
    send_grad = (slot_weight[:, None] * picked_grad).astype(jnp.bfloat16)
    got_rows, got_grad = (
        lax.all_to_all(
            send_rows.reshape(experts, CAP, width),
            "expert",
            split_axis=0,
            concat_axis=0,
            tiled=True,
        ),
        lax.all_to_all(
            send_grad.reshape(experts, CAP, width),
            "expert",
            split_axis=0,
            concat_axis=0,
            tiled=True,
        ),
    )
    rows_in = got_rows.reshape(slots, width)
    pick_grad = got_grad.reshape(slots, width)
    first = w_gate_up[0]
    second = w_down[0]
    partial_value = jnp.einsum("rk,kcf->rcf", rows_in, first, preferred_element_type=jnp.float32)
    pre = reduce_width(partial_value)
    gate, upper, sig, act, hidden_share = forward_share(pre)
    hidden = spread_back(hidden_share)[:, 0, :]
    expert_out = jnp.dot(hidden, second, preferred_element_type=jnp.float32).astype(jnp.bfloat16)
    back_out = lax.all_to_all(
        expert_out.reshape(experts, CAP, width), "expert", split_axis=0, concat_axis=0, tiled=True
    )
    grad_second = jnp.einsum(
        "rf,rk->fk", hidden, pick_grad, preferred_element_type=jnp.float32
    ).astype(jnp.bfloat16)
    grad_partial = jnp.einsum("rk,fk->rf", pick_grad, second, preferred_element_type=jnp.float32)[
        :, None, :
    ]
    grad_hidden = reduce_width(grad_partial)[:, 0, :]
    grad_share = backward_share(grad_hidden, gate, upper, sig, act)
    grad_pre = spread_back(grad_share)
    grad_first = jnp.einsum(
        "rk,rcf->kcf", rows_in, grad_pre, preferred_element_type=jnp.float32
    ).astype(jnp.bfloat16)
    pick_dx = jnp.einsum("rcf,kcf->rk", grad_pre, first, preferred_element_type=jnp.float32).astype(
        jnp.bfloat16
    )
    back_dx = lax.all_to_all(
        pick_dx.reshape(experts, CAP, width), "expert", split_axis=0, concat_axis=0, tiled=True
    )
    slot_index = jnp.clip(target, 0, slots - 1)
    returned = back_out.reshape(slots, width)[slot_index]
    pick_weight = jnp.where(kept, combine, jnp.float32(0.0))
    layer_out = jnp.sum(pick_weight[:, :, None] * returned.astype(jnp.float32), axis=1).astype(
        jnp.bfloat16
    )
    grad_tokens = jnp.dot(
        place.T, back_dx.reshape(slots, width), preferred_element_type=jnp.float32
    ).astype(jnp.bfloat16)
    return (layer_out, grad_tokens, grad_first[None], grad_second[None])


def solution(mesh):
    placed = (
        P("expert", "dp"),
        P("expert", "dp"),
        P("expert", None),
        P("expert", None),
        P("expert", "dp", None, None),
        P("expert", None, "dp"),
    )
    return jax.shard_map(
        body,
        mesh=mesh,
        in_specs=placed,
        out_specs=(
            P("expert", "dp"),
            P("expert", "dp"),
            P("expert", "dp", None, None),
            P("expert", None, "dp"),
        ),
        check_vma=False,
    )
```

profile of v0, /device:TPU:1, one launch (start us, length us, event | category | flops | bytes accessed | tf_op | source)
XLA Modules:
  0.0 631.0 jit_solution(9032483214978329246)
XLA Ops:
  7.2 0.0 reduce-scatter.5.cloned.1.call-start
  7.3 0.9 copy.50
  8.2 0.1 eq.43
  8.3 0.1 eq.39
  8.4 9.1 %reduce-window.6 = s32[32,12,128]{2,1,0:T(8,128)S(1)} reduce-window(s32[32,12,128]{2,1,0:T(8,128)S(1)} %fusion.20, s32[]{:T(128)} %constant.4.clone.1), window={size=1x1x128 pad=0_0x0_0x127_0}, to_apply=%region_1.0 | reduce-window | flops 6242304 | bytes 393220 | tf_op jit(solution)/shard_map/reduce-window
  17.5 0.1 slice.18
  17.6 0.2 copy.52
  17.9 0.1 copy.53
  18.0 0.1 broadcast_add_fusion
  18.1 0.1 fusion.23
  18.2 0.1 reshape.59
  18.3 0.1 copy.54
  18.4 0.1 copy.55
  18.5 0.1 copy.58
  18.6 2.6 select_reduce_fusion
  21.2 0.3 fusion.11
  21.6 28.6 %all_to_all.20 = bf16[32,24,128]{2,1,0:T(8,128)(2,1)S(1)} all-to-all(bf16[32,24,128]{2,1,0:T(8,128)(2,1)S(1)} %bitcast.81), channel_id=1, replica_groups=mesh['expert'=32,'dp'=32] {'expert'}, dimensions={0} | all-to-all | bytes 393216 | tf_op jit(solution)/shard_map/all_to_all | solution.py:59
  50.2 1.9 convolution_bitcast_fusion
  52.1 0.0 reduce-scatter.5.cloned.1.call-update
  52.1 0.0 reduce-scatter.3.cloned.1.call-start
  52.2 0.3 convolution_convert_fusion.1
  52.5 16.3 %all_to_all.21 = bf16[32,24,128]{2,1,0:T(8,128)(2,1)S(1)} all-to-all(bf16[32,24,128]{2,1,0:T(8,128)(2,1)S(1)} %bitcast.82), channel_id=1, replica_groups=mesh['expert'=32,'dp'=32] {'expert'}, dimensions={0} | all-to-all | bytes 393216 | tf_op jit(solution)/shard_map/all_to_all | solution.py:52
  68.8 2.9 fusion.18
  71.7 0.0 reduce-scatter.3.cloned.1.call-update
  71.7 0.0 all-gather.3.cloned.1.call-start
  71.7 97.0 %reduce-scatter.5.cloned.1.call-done = f32[24,1,768]{2,0,1:T(8,128)} async-done(((f32[768,1,768]{2,0,1:T(8,128)}), f32[24,1,768]{2,0,1:T(8,128)}) %reduce-scatter.5.cloned.1.call-update) | async-done | bytes 73744 | tf_op jit(solution)/shard_map/reduce_scatter | solution.py:10
  168.8 144.7 %reduce-scatter.3.cloned.1.call-done = f32[24,2,768]{2,0,1:T(8,128)} async-done(((f32[768,2,768]{2,0,1:T(8,128)}), f32[24,2,768]{2,0,1:T(8,128)}) %reduce-scatter.3.cloned.1.call-update) | async-done | bytes 147472 | tf_op jit(solution)/shard_map/reduce_scatter | solution.py:10
  313.4 1.6 multiply_convert_fusion.1
  315.1 0.0 all-gather.3.cloned.1.call-update
  315.1 0.0 all-gather.5.cloned.1.call-start
  315.1 0.6 pad_maximum_fusion
  315.8 127.3 %all-gather.3.cloned.1.call-done = bf16[768,1,768]{2,0,1:T(8,128)(2,1)} async-done(((bf16[24,1,768]{2,0,1:T(8,128)(2,1)}), bf16[768,1,768]{2,0,1:T(8,128)(2,1)}) %all-gather.3.cloned.1.call-update) | async-done | bytes 1179664 | tf_op jit(solution)/shard_map/all_gather | solution.py:14
  443.1 2.5 fusion.5
  445.6 31.8 %all-to-all-start.1 = ((bf16[32,24,128]{2,1,0:T(8,128)(2,1)}), bf16[32,24,128]{2,1,0:T(8,128)(2,1)S(1)}, u32[]{:S(2)}, u32[]{:S(2)}) async-start(bf16[32,24,128]{2,1,0:T(8,128)(2,1)} %bitcast.8), calls=%async_computation.2 | async-start | bytes 393216 | tf_op jit(solution)/shard_map/all_to_all | solution.py:76
  477.4 0.1 copy.57
  477.5 0.1 reshape.70
  477.6 0.1 copy.49
  477.8 1.2 fusion.13
  479.0 10.1 %all-to-all-done.1 = bf16[32,24,128]{2,1,0:T(8,128)(2,1)S(1)} async-done(((bf16[32,24,128]{2,1,0:T(8,128)(2,1)}), bf16[32,24,128]{2,1,0:T(8,128)(2,1)S(1)}, u32[]{:S(2)}, u32[]{:S(2)}) %all-to-all-start.1) | async-done | bytes 196640 | tf_op jit(solution)/shard_map/all_to_all | solution.py:76
  489.1 4.1 gather_fusion
  493.2 84.4 %all-gather.5.cloned.1.call-done = bf16[768,2,768]{2,0,1:T(8,128)(2,1)} async-done(((bf16[24,2,768]{2,0,1:T(8,128)(2,1)}), bf16[768,2,768]{2,0,1:T(8,128)(2,1)}) %all-gather.5.cloned.1.call-update) | async-done | bytes 2359312 | tf_op jit(solution)/shard_map/all_gather | solution.py:14
  577.6 3.3 fusion.12
  580.9 31.1 %all-to-all-start.3 = ((bf16[32,24,128]{2,1,0:T(8,128)(2,1)}), bf16[32,24,128]{2,1,0:T(8,128)(2,1)S(1)}, u32[]{:S(2)}, u32[]{:S(2)}) async-start(bf16[32,24,128]{2,1,0:T(8,128)(2,1)} %bitcast.83), calls=%async_computation.5 | async-start | bytes 393216 | tf_op jit(solution)/shard_map/all_to_all | solution.py:94
  612.0 1.9 fusion.16
  613.9 0.5 fusion
  614.4 1.2 copy.61
  615.5 8.1 %all-to-all-done.3 = bf16[32,24,128]{2,1,0:T(8,128)(2,1)S(1)} async-done(((bf16[32,24,128]{2,1,0:T(8,128)(2,1)}), bf16[32,24,128]{2,1,0:T(8,128)(2,1)S(1)}, u32[]{:S(2)}, u32[]{:S(2)}) %all-to-all-start.3) | async-done | bytes 196640 | tf_op jit(solution)/shard_map/all_to_all | solution.py:94
  623.7 0.8 convolution_convert_fusion.2
  (23 shorter events, 0.2 us)
Async XLA Ops:
  7.2 61.6 %copy-start = (bf16[1,128,2,768]{3,2,1,0:T(2,128)(2,1)S(1)}, bf16[1,128,2,768]{3,2,1,0:T(2,128)(2,1)}, u32[]{:S(2)}) copy-start(bf16[1,128,2,768]{3,2,1,0:T(2,128)(2,1)} %param.10) | copy-start | bytes 1179652
  7.2 11.2 %copy-start.4 = (s32[192,8]{0,1:T(8,128)S(1)}, s32[192,8]{0,1:T(8,128)}, u32[]{:S(2)}) copy-start(s32[192,8]{0,1:T(8,128)} %param.8) | copy-start | bytes 18436
  7.2 11.3 %copy-start.7 = (f32[192,8]{0,1:T(8,128)S(1)}, f32[192,8]{0,1:T(8,128)}, u32[]{:S(2)}) copy-start(f32[192,8]{0,1:T(8,128)} %param.9) | copy-start | bytes 18436
  7.2 14.0 %copy-start.5 = (bf16[192,128]{1,0:T(8,128)(2,1)S(1)}, bf16[192,128]{1,0:T(8,128)(2,1)}, u32[]{:S(2)}) copy-start(bf16[192,128]{1,0:T(8,128)(2,1)} %param.7) | copy-start | bytes 147460
  7.2 43.0 %copy-start.3 = (bf16[1,768,128]{2,1,0:T(8,128)(2,1)S(1)}, bf16[1,768,128]{2,1,0:T(8,128)(2,1)}, u32[]{:S(2)}) copy-start(bf16[1,768,128]{2,1,0:T(8,128)(2,1)} %param.11) | copy-start | bytes 589828
  7.2 161.6 %reduce-scatter.5.cloned.1.call-start = ((), (), s32[]{:S(2)}) async-start(), calls=%async_computation.8 | async-start | bytes 2433024 | tf_op jit(solution)/shard_map/reduce_scatter | solution.py:10
  50.2 2.0 copy-start.6
  52.1 261.4 %reduce-scatter.3.cloned.1.call-start = ((), (), s32[]{:S(2)}) async-start(), calls=%async_computation.6 | async-start | bytes 4866048 | tf_op jit(solution)/shard_map/reduce_scatter | solution.py:10
  71.7 371.4 %all-gather.3.cloned.1.call-start = ((), (), s32[]{:S(2)}) async-start(), calls=%async_computation.7 | async-start | bytes 1216512 | tf_op jit(solution)/shard_map/all_gather | solution.py:14
  315.1 262.5 %all-gather.5.cloned.1.call-start = ((), (), s32[]{:S(2)}) async-start(), calls=%async_computation.9 | async-start | bytes 2433024 | tf_op jit(solution)/shard_map/all_gather | solution.py:14
  443.1 34.7 %copy-start.1 = (bf16[768,1,768]{2,0,1:T(8,128)(2,1)S(1)}, bf16[768,1,768]{2,0,1:T(8,128)(2,1)}, u32[]{:S(2)}) copy-start(bf16[768,1,768]{2,0,1:T(8,128)(2,1)} %all-gather.3.cloned.1.call-done) | copy-start | bytes 3538948
  445.6 43.5 %all-to-all-start.1 = ((bf16[32,24,128]{2,1,0:T(8,128)(2,1)}), bf16[32,24,128]{2,1,0:T(8,128)(2,1)S(1)}, u32[]{:S(2)}, u32[]{:S(2)}) async-start(bf16[32,24,128]{2,1,0:T(8,128)(2,1)} %bitcast.8), calls=%async_computation.2 | async-start | bytes 393216 | tf_op jit(solution)/shard_map/all_to_all | solution.py:76
  577.6 36.3 %copy-start.2 = (bf16[768,2,768]{2,0,1:T(8,128)(2,1)S(1)}, bf16[768,2,768]{2,0,1:T(8,128)(2,1)}, u32[]{:S(2)}) copy-start(bf16[768,2,768]{2,0,1:T(8,128)(2,1)} %all-gather.5.cloned.1.call-done) | copy-start | bytes 7077892
  580.9 42.8 %all-to-all-start.3 = ((bf16[32,24,128]{2,1,0:T(8,128)(2,1)}), bf16[32,24,128]{2,1,0:T(8,128)(2,1)S(1)}, u32[]{:S(2)}, u32[]{:S(2)}) async-start(bf16[32,24,128]{2,1,0:T(8,128)(2,1)} %bitcast.83), calls=%async_computation.5 | async-start | bytes 393216 | tf_op jit(solution)/shard_map/all_to_all | solution.py:94
Sparse Core Ops, SparseCore 0:
  52.2 116.5 reduce-scatter.4
  172.2 141.2 reduce-scatter.2
  316.7 126.3 all-gather.2
  445.6 131.9 all-gather.4
where the time goes:
time: 632 us; the launch traced here: 631 us
  waiting for transfers between devices  472 us (75%)
  starting transfers between devices  63 us (10%)
  blocking collectives  44.9 us (7%)
  other arithmetic  16.1 us (3%)
  between operations  14 us (2%)
  matrix products  13.7 us (2%)
  local copies, waits for them, and re-layouts  7.46 us (1%)
    reduce_scatter x2, waiting for transfers between devices, reduce_width(): lax.psum_scatter(partial_value, 'dp', scatter_dimension=0, tiled=True)  242 us
    all_gather x2, waiting for transfers between devices, spread_back(): return lax.all_gather(share, 'dp', axis=0, tiled=True)  212 us
    all_to_all x1, starting transfers between devices, body(): lax.all_to_all(expert_out.reshape(experts, CAP, width), 'expert', split_a...  31.8 us
    all_to_all x1, starting transfers between devices, body(): lax.all_to_all(pick_dx.reshape(experts, CAP, width), 'expert', split_axis...  31.1 us
    all_to_all x1, blocking collectives, body(): lax.all_to_all(send_grad.reshape(experts, CAP, width), 'expert', split_ax...  28.6 us
    all_to_all x1, blocking collectives, body(): lax.all_to_all(send_rows.reshape(experts, CAP, width), 'expert', split_ax...  16.3 us
  transfers between devices with their start and end apart: 6, of which 6 were waited for; matrix products, arithmetic and copies ran while one was open for 2% of the time, Pallas kernels for 0%

commit v1 on v0

v1 whole, which is shorter than its diff:
```python
import functools

import jax
import jax.numpy as jnp
import numpy as np
from jax import lax
from jax.experimental import pallas as pl
from jax.experimental.pallas import tpu as pltpu
from jax.sharding import PartitionSpec as P

CAP = 24
BLK = 2 * CAP
GROUPS = 4
MSG = jnp.float32
MESH = pl.DeviceIdType.MESH
BF = jnp.bfloat16
F32 = jnp.float32


def dot(a, b, ca, cb):
    return lax.dot_general(a, b, (((ca,), (cb,)), ((), ())), preferred_element_type=F32)


def landed(ref, sem):
    pltpu.make_async_copy(ref, ref, sem).wait()


def kernel(
    ne, nz, routes, scores, tokens, ograd, wgu, wd, slot, lower,
    out, gtok, ggu, gdn,
    place, whi, wlo, disp, rbuf, rows, grads, wgu2, wdp, part,
    s_up, r_up, s_dn, r_dn, hid, gp, xo_s, xo_r, own, cb_s, cb_r, tg_u, tg_d,
    d_send, d_recv, w_send, w_recv, f_send, f_recv,
    ru_send, ru_recv, rd_send, rd_recv, gu_send, gu_recv, gd_send, gd_recv,
    o_send, o_recv, c_send, c_recv, t_send, t_recv,
):
    e = lax.axis_index("expert")
    dp = lax.axis_index("dp")
    b = dp // nz
    z = lax.rem(dp, nz)
    side = (1 - b) * nz + z
    above = b * nz + lax.rem(z + 1, nz)
    below = b * nz + lax.rem(z + nz - 1, nz)
    slots = ne * CAP
    width = tokens.shape[1]
    half = wd.shape[1]
    share = slots // nz
    n_up, n_dn = nz // 2, nz // 2 - 1
    chunks = [(0, 2 * half), (2 * half, 3 * half)]
    per = ne // GROUPS

    def far(src, dst, send, recv, to_e, to_dp):
        return pltpu.make_async_remote_copy(
            src_ref=src, dst_ref=dst, send_sem=send, recv_sem=recv,
            device_id=(to_e, to_dp), device_id_type=MESH,
        )

    barrier = pltpu.get_barrier_semaphore()

    def greet(i, c):
        pl.semaphore_signal(
            barrier, inc=1, device_id=(lax.rem(e + i, ne), dp), device_id_type=MESH
        )
        return c

    lax.fori_loop(1, ne, greet, 0)
    for to in (side, above, below):
        pl.semaphore_signal(barrier, inc=1, device_id=(e, to), device_id_type=MESH)

    combine = scores[...] / jnp.sum(scores[...], axis=1, keepdims=True)
    slot_e, slot_r = slot[0:1, :], slot[1:2, :]
    tok = tokens.shape[0]
    hit = jnp.zeros((tok, slots), F32)
    weight = jnp.zeros((tok, slots), F32)
    for j in range(routes.shape[1]):
        named = routes[:, j : j + 1] == slot_e
        hit = jnp.where(named, 1.0, hit)
        weight = jnp.where(named, combine[:, j : j + 1], weight)
    rank = dot(lower[...], hit.astype(BF), 1, 0)
    taken = jnp.where(rank == slot_r.astype(F32), hit, 0.0)
    weight = weight * taken
    place[...] = taken.astype(BF)
    high = weight.astype(BF)
    whi[...] = high
    wlo[...] = (weight - high.astype(F32)).astype(BF)
    send_rows = dot(place[...], tokens[...], 0, 0)
    send_grad = dot(whi[...], ograd[...], 0, 0) + dot(wlo[...], ograd[...], 0, 0)
    both = jnp.concatenate(
        [send_rows.reshape(ne, CAP, width), send_grad.reshape(ne, CAP, width)], axis=1
    )
    disp[...] = both.reshape(ne * BLK, width).astype(BF)
    pl.semaphore_wait(barrier, ne + 2)

    def block(i):
        return pl.ds(pl.multiple_of(i * BLK, BLK), BLK)

    def dispatch(i, c):
        to = lax.rem(e + i, ne)
        far(disp.at[block(to)], rbuf.at[0, block(e)], d_send, d_recv.at[e // per], to, dp).start()
        return c

    lax.fori_loop(1, ne, dispatch, 0)
    pltpu.make_async_copy(disp.at[block(e)], rbuf.at[0, block(e)], d_recv.at[e // per]).start()

    w1 = far(wgu.at[1 - b], wgu2.at[pl.ds(width, width)], w_send.at[0], w_recv.at[0], e, side)
    w2 = far(wd.at[1 - b], wdp, w_send.at[1], w_recv.at[1], e, side)
    w1.start()
    w2.start()
    wgu2[0:width, :] = wgu[b]

    grp = per * BLK
    forward = []
    for g in range(GROUPS):
        at = pl.ds(g * grp, grp)
        landed(rbuf.at[0, at], d_recv.at[g])
        move = far(rbuf.at[0, at], rbuf.at[1, at], f_send.at[g], f_recv.at[g], e, side)
        move.start()
        forward.append(move)

    def unpack(which):
        got = rbuf[which].astype(F32).reshape(ne, BLK, width)
        cols = slice(which * width, (which + 1) * width)
        rows[:, cols] = got[:, :CAP].reshape(slots, width).astype(BF)
        grads[:, cols] = got[:, CAP:].reshape(slots, width).astype(BF)

    unpack(0)
    w1.wait_recv()
    w2.wait_recv()
    for move in forward:
        move.wait_recv()
    unpack(1)

    step = slots // 4
    wd2 = jnp.concatenate([wd[b], wdp[...]], axis=1)

    def partial(i, c):
        at = pl.ds(pl.multiple_of(i * step, step), step)
        part[at, 0 : 2 * half] = dot(rows[at, :], wgu2[...], 1, 0)
        part[at, 2 * half : 3 * half] = dot(grads[at, :], wd2, 1, 1)
        return c

    lax.fori_loop(0, 4, partial, 0)

    def of(d):
        return pl.ds(pl.multiple_of(d * share, share), share)

    def sum_up(k, first):
        d = lax.rem(z + n_up - k, nz)
        for c, (lo, hi) in enumerate(chunks):
            value = part[of(d), lo:hi]
            if not first:
                landed(r_up.at[k - 1, :, lo:hi], ru_recv.at[k - 1, c])
                value = value + r_up[k - 1, :, lo:hi].astype(F32)
            s_up[k, :, lo:hi] = value.astype(MSG)
            far(
                s_up.at[k, :, lo:hi], r_up.at[k, :, lo:hi],
                ru_send.at[k, c], ru_recv.at[k, c], e, above,
            ).start()

    def sum_dn(k, first):
        d = lax.rem(z + nz - n_dn + k, nz)
        for c, (lo, hi) in enumerate(chunks):
            value = part[of(d), lo:hi]
            if not first:
                landed(r_dn.at[k - 1, :, lo:hi], rd_recv.at[k - 1, c])
                value = value + r_dn[k - 1, :, lo:hi].astype(F32)
            s_dn[k, :, lo:hi] = value.astype(MSG)
            far(
                s_dn.at[k, :, lo:hi], r_dn.at[k, :, lo:hi],
                rd_send.at[k, c], rd_recv.at[k, c], e, below,
            ).start()

    sum_up(0, True)
    sum_dn(0, True)

    def hop(k, c):
        sum_up(k, False)
        sum_dn(k, False)
        return c

    lax.fori_loop(1, n_dn, hop, 0)
    sum_up(n_up - 1, False)
    total = []
    for c, (lo, hi) in enumerate(chunks):
        landed(r_dn.at[n_dn - 1, :, lo:hi], rd_recv.at[n_dn - 1, c])
        landed(r_up.at[n_up - 1, :, lo:hi], ru_recv.at[n_up - 1, c])
        total.append(
            part[of(z), lo:hi]
            + r_up[n_up - 1, :, lo:hi].astype(F32)
            + r_dn[n_dn - 1, :, lo:hi].astype(F32)
        )
    gate, upper, grad_hidden = total[0][:, :half], total[0][:, half:], total[1]
    sig = jax.nn.sigmoid(gate)
    act = gate * sig
    hid[of(z), :] = (act * upper).astype(BF)
    gp[of(z), 0:half] = (grad_hidden * upper * sig * (1.0 + gate * (1.0 - sig))).astype(BF)
    gp[of(z), half : 2 * half] = (grad_hidden * act).astype(BF)

    def pass_on(k, first, way):
        d = lax.rem(z + nz - k, nz) if way else lax.rem(z + k, nz)
        send, recv, to = (gu_send, gu_recv, above) if way else (gd_send, gd_recv, below)
        for c, ref in enumerate((hid, gp)):
            if not first:
                landed(ref.at[of(d)], recv.at[k - 1, c])
            far(ref.at[of(d)], ref.at[of(d)], send.at[k, c], recv.at[k, c], e, to).start()

    pass_on(0, True, True)
    pass_on(0, True, False)

    def relay(k, c):
        pass_on(k, False, True)
        pass_on(k, False, False)
        return c

    lax.fori_loop(1, n_dn, relay, 0)
    pass_on(n_up - 1, False, True)
    for c, ref in enumerate((hid, gp)):
        landed(ref.at[of(lax.rem(z + n_dn, nz))], gd_recv.at[n_dn - 1, c])
        landed(ref.at[of(lax.rem(z + nz - n_up, nz))], gu_recv.at[n_up - 1, c])

    def spread(i, c):
        at = pl.ds(pl.multiple_of(i * step, step), step)
        eo = dot(hid[at, :], wd2, 1, 0)
        own[0, at, :] = eo[:, :width]
        xo_s[0, at, :] = eo[:, width:].astype(BF)
        dx = dot(gp[at, :], wgu2[...], 1, 1)
        own[1, at, :] = dx[:, :width]
        xo_s[1, at, :] = dx[:, width:].astype(BF)
        return c

    lax.fori_loop(0, 4, spread, 0)
    cross = []
    for i in range(2):
        move = far(xo_s.at[i], xo_r.at[i], o_send.at[i], o_recv.at[i], e, side)
        move.start()
        cross.append(move)
    gg = dot(rows[...], gp[...], 0, 0)
    tg_u[...] = gg[width:].astype(BF)
    t1 = far(tg_u, ggu.at[b], t_send.at[0], t_recv.at[0], e, side)
    t1.start()
    ggu[b] = gg[:width].astype(BF)
    gd = dot(hid[...], grads[...], 0, 0)
    tg_d[...] = gd[:, width:].astype(BF)
    t2 = far(tg_d, gdn.at[b], t_send.at[1], t_recv.at[1], e, side)
    t2.start()
    gdn[b] = gd[:, :width].astype(BF)

    for move in cross:
        move.wait_recv()
    back = [
        (own[i] + xo_r[i].astype(F32)).reshape(ne, CAP, width) for i in range(2)
    ]
    cb_s[...] = jnp.concatenate(back, axis=1).reshape(ne * BLK, width).astype(BF)

    def give_back(i, c):
        to = lax.rem(e + i, ne)
        far(cb_s.at[block(to)], cb_r.at[block(e)], c_send, c_recv, to, dp).start()
        return c

    lax.fori_loop(1, ne, give_back, 0)
    pltpu.make_async_copy(cb_s.at[block(e)], cb_r.at[block(e)], c_recv).start()
    landed(cb_r, c_recv)
    got = cb_r[...].astype(F32).reshape(ne, BLK, width)
    eo = got[:, :CAP].reshape(slots, width).astype(BF)
    dx = got[:, CAP:].reshape(slots, width).astype(BF)
    out[...] = (dot(whi[...], eo, 1, 0) + dot(wlo[...], eo, 1, 0)).astype(BF)
    gtok[...] = dot(place[...], dx, 1, 0).astype(BF)

    t1.wait_recv()
    t2.wait_recv()
    sent = pl.ds(0, (ne - 1) * BLK)
    landed(disp.at[sent], d_send)
    landed(cb_s.at[sent], c_send)
    for move in (w1, w2, *forward, *cross, t1, t2):
        move.wait_send()
    for send, ring, n in ((ru_send, s_up, n_up), (rd_send, s_dn, n_dn)):
        for k in range(n):
            for c, (lo, hi) in enumerate(chunks):
                landed(ring.at[k, :, lo:hi], send.at[k, c])
    for send, n in ((gu_send, n_up), (gd_send, n_dn)):
        for k in range(n):
            for c, ref in enumerate((hid, gp)):
                landed(ref.at[pl.ds(0, share)], send.at[k, c])


def body(tokens, out_grad, routes, scores, w_gate_up, w_down):
    ne, ndp = lax.axis_size("expert"), lax.axis_size("dp")
    nz = ndp // 2
    tok, width = tokens.shape
    hidden = w_down.shape[1]
    half = hidden // 2
    slots = ne * CAP
    share = slots // nz
    n_up, n_dn = nz // 2, nz // 2 - 1
    ids = np.arange(slots)
    slot = jnp.asarray(np.stack([ids // CAP, ids % CAP]).astype(np.int32))
    lower = jnp.asarray(np.tril(np.ones((tok, tok), np.float32), -1)).astype(BF)
    wgu = w_gate_up[0].reshape(width, 2, 2, half).transpose(2, 0, 1, 3).reshape(2, width, 2 * half)
    wd = w_down[0].reshape(2, half, width)
    dma = pltpu.SemaphoreType.DMA
    out, gtok, ggu, gdn = pl.pallas_call(
        functools.partial(kernel, ne, nz),
        out_shape=(
            jax.ShapeDtypeStruct((tok, width), BF),
            jax.ShapeDtypeStruct((tok, width), BF),
            jax.ShapeDtypeStruct((2, width, 2 * half), BF),
            jax.ShapeDtypeStruct((2, half, width), BF),
        ),
        in_specs=[pl.BlockSpec(memory_space=pltpu.VMEM)] * 8,
        out_specs=[pl.BlockSpec(memory_space=pltpu.VMEM)] * 4,
        scratch_shapes=[
            pltpu.VMEM((tok, slots), BF),
            pltpu.VMEM((tok, slots), BF),
            pltpu.VMEM((tok, slots), BF),
            pltpu.VMEM((ne * BLK, width), BF),
            pltpu.VMEM((2, ne * BLK, width), BF),
            pltpu.VMEM((slots, 2 * width), BF),
            pltpu.VMEM((slots, 2 * width), BF),
            pltpu.VMEM((2 * width, 2 * half), BF),
            pltpu.VMEM((half, width), BF),
            pltpu.VMEM((slots, 3 * half), F32),
            pltpu.VMEM((n_up, share, 3 * half), MSG),
            pltpu.VMEM((n_up, share, 3 * half), MSG),
            pltpu.VMEM((n_dn, share, 3 * half), MSG),
            pltpu.VMEM((n_dn, share, 3 * half), MSG),
            pltpu.VMEM((slots, half), BF),
            pltpu.VMEM((slots, 2 * half), BF),
            pltpu.VMEM((2, slots, width), BF),
            pltpu.VMEM((2, slots, width), BF),
            pltpu.VMEM((2, slots, width), F32),
            pltpu.VMEM((ne * BLK, width), BF),
            pltpu.VMEM((ne * BLK, width), BF),
            pltpu.VMEM((width, 2 * half), BF),
            pltpu.VMEM((half, width), BF),
            dma, dma((GROUPS,)),
            dma((2,)), dma((2,)),
            dma((GROUPS,)), dma((GROUPS,)),
            dma((n_up, 2)), dma((n_up, 2)), dma((n_dn, 2)), dma((n_dn, 2)),
            dma((n_up, 2)), dma((n_up, 2)), dma((n_dn, 2)), dma((n_dn, 2)),
            dma((2,)), dma((2,)),
            dma, dma,
            dma((2,)), dma((2,)),
        ],
        compiler_params=pltpu.CompilerParams(
            collective_id=0, has_side_effects=True, vmem_limit_bytes=48 * 1024 * 1024
        ),
    )(routes, scores, tokens, out_grad, wgu, wd, slot, lower)
    grad_first = (
        ggu.reshape(2, width, 2, half).transpose(1, 2, 0, 3).reshape(1, width, 2, hidden)
    )
    return out, gtok, grad_first, gdn.reshape(1, hidden, width)


def solution(mesh):
    placed = (
        P("expert", "dp"),
        P("expert", "dp"),
        P("expert", None),
        P("expert", None),
        P("expert", "dp", None, None),
        P("expert", None, "dp"),
    )
    return jax.shard_map(
        body,
        mesh=mesh,
        in_specs=placed,
        out_specs=(
            P("expert", "dp"),
            P("expert", "dp"),
            P("expert", "dp", None, None),
            P("expert", None, "dp"),
        ),
        check_vma=False,
    )
```

time: 632 us -> 148 us (0.23)
  waiting for transfers between devices: 472 us -> 0 us
  Pallas kernels: 0 us -> 140 us
  starting transfers between devices: 63 us -> 0 us
  blocking collectives: 44.9 us -> 0 us
  other arithmetic: 16.1 us -> 0 us
  matrix products: 13.7 us -> 0 us
  between operations: 14 us -> 0.74 us
    reduce_scatter x2 -> x0, waiting for transfers between devices: 242 us -> none  [reduce_width(): lax.psum_scatter(partial_value, 'dp', scatter_dimension=0, tiled=True)]
    all_gather x2 -> x0, waiting for transfers between devices: 212 us -> none  [spread_back(): return lax.all_gather(share, 'dp', axis=0, tiled=True)]
    pallas_call x0 -> x1, Pallas kernels: none -> 140 us  [body(): pl.pallas_call(functools.partial(kernel, ne, nz), out_shape=(jax.ShapeDty...]
    all_to_all x2 -> x0, starting transfers between devices: 62.8 us -> none  [the longest x1 31.8 us: body(): lax.all_to_all(expert_out.reshape(experts, CAP, width), 'expert', split_a...]
    all_to_all x2 -> x0, blocking collectives: 44.9 us -> none  [the longest x1 28.6 us: body(): lax.all_to_all(send_grad.reshape(experts, CAP, width), 'expert', split_ax...]
    all_to_all x2 -> x0, waiting for transfers between devices: 18.3 us -> none  [the longest x1 10.1 us: body(): lax.all_to_all(expert_out.reshape(experts, CAP, width), 'expert', split_a...]
    dot_general x9 -> x0, matrix products: 13.7 us -> none  [the longest x1 3.27 us: body(): jnp.einsum('rcf,kcf->rk', grad_pre, first, preferred_element_type=jnp.flo...]
    another operation x5 -> x0, other arithmetic: 11.5 us -> none
  transfers between devices with their start and end apart: 6 -> 0, of which waited for: 6 -> 0; matrix products, arithmetic and copies ran while one was open for 2% -> 0% of each run, Pallas kernels for 0% -> 0%
where the time goes in v1:
time: 148 us
  Pallas kernels  140 us (95%)
  local copies, waits for them, and re-layouts  7.04 us (5%)
    pallas_call x1, Pallas kernels, body(): pl.pallas_call(functools.partial(kernel, ne, nz), out_shape=(jax.ShapeDty...  140 us
    unnamed x17, local copies, waits for them, and re-layouts  3.54 us

profile of v1, /device:TPU:1, one launch (start us, length us, event | category | flops | bytes accessed | tf_op | source)
XLA Modules:
  0.0 147.8 jit_solution(11425421660115460410)
XLA Ops:
  0.6 0.0 copy-start.5
  0.6 0.8 copy.13.routes
  1.5 0.0 copy-done.5
  1.5 0.1 copy.14.scores
  1.6 1.3 reshape_squeeze.6
  2.8 0.3 copy.17
  3.1 0.0 copy-start
  3.2 0.0 copy-start.1
  3.2 0.0 copy-start.2
  3.2 0.0 copy-start.3
  3.2 0.0 copy-start.4
  3.2 0.2 reshape.20.wgu
  3.5 0.6 copy-done
  4.1 0.1 copy-done.1
  4.1 0.0 copy-done.2
  4.1 0.0 copy-done.3
  4.1 0.0 copy-done.4
  4.1 140.0 %shard_map.111 = (bf16[192,128]{1,0:T(8,128)(2,1)S(1)}, bf16[192,128]{1,0:T(8,128)(2,1)S(1)}, bf16[2,128,768]{2,1,0:T(8,128)(2,1)S(1)}, bf16[2,384,128]{2,1,0:T(8,128)(2,1)S(1)}) custom-call(s32[192,8]{1,0:T(8,128)S(1)} %copy.13.routes, f32[192,8]{1,0:T(8,128)S(1)} %copy.14.scores, bf16[192,128]{1,0:T(8,128)(2,1)S(1)} %copy-done.2, ...), custom_call_target="tpu_custom_call" | custom-call | tf_op jit(solution)/shard_map/pallas_call | solution.py:301
  144.2 0.1 reshape.21
  144.3 0.6 copy.15
  144.9 1.0 reshape.22
  145.9 0.6 copy.21
  146.5 0.6 copy.22
  147.1 0.7 copy.23
Async XLA Ops:
  0.6 0.8 copy-start.5
  3.1 0.9 copy-start
  3.2 1.0 copy-start.1
  3.2 1.0 copy-start.2
  3.2 1.0 copy-start.3
  3.2 1.0 copy-start.4

commit v2 on v1

v2 whole, which is shorter than its diff:
```python
import functools

import jax
import jax.numpy as jnp
import numpy as np
from jax import lax
from jax.experimental import pallas as pl
from jax.experimental.pallas import tpu as pltpu
from jax.sharding import PartitionSpec as P

CAP = 24
BLK = 2 * CAP
GROUPS = 8
WIDE = 2
MESH = pl.DeviceIdType.MESH
BF = jnp.bfloat16
F32 = jnp.float32


def dot(a, b, ca, cb):
    return lax.dot_general(a, b, (((ca,), (cb,)), ((), ())), preferred_element_type=F32)


def landed(ref, sem):
    pltpu.make_async_copy(ref, ref, sem).wait()


def kernel(
    ne, nz, routes, scores, tokens, ograd, wgu, wd, slot, lower,
    out, gtok, ggu, gdn,
    place, whi, wlo, disp, rbuf, rows, grads, wgu2, wdp, part,
    su_n, ru_n, su_w, ru_w, sd_n, rd_n, sd_w, rd_w,
    act, xo_s, xo_r, own, cb_s, cb_r, tg_u, tg_d, acc_u, acc_d,
    d_send, d_recv, w_send, w_recv, f_send, f_recv,
    ru_send, ru_recv, rd_send, rd_recv, gu_send, gu_recv, gd_send, gd_recv,
    o_send, o_recv, c_send, c_recv, t_send, t_recv,
):
    e = lax.axis_index("expert")
    dp = lax.axis_index("dp")
    b = dp // nz
    z = lax.rem(dp, nz)
    side = (1 - b) * nz + z
    above = b * nz + lax.rem(z + 1, nz)
    below = b * nz + lax.rem(z + nz - 1, nz)
    slots = ne * CAP
    width = tokens.shape[1]
    half = wd.shape[1]
    share = slots // nz
    n_up, n_dn = nz // 2, nz // 2 - 1
    narrow = max(1, n_up - WIDE)
    per = ne // GROUPS

    def far(src, dst, send, recv, to_e, to_dp):
        return pltpu.make_async_remote_copy(
            src_ref=src, dst_ref=dst, send_sem=send, recv_sem=recv,
            device_id=(to_e, to_dp), device_id_type=MESH,
        )

    barrier = pltpu.get_barrier_semaphore()

    def greet(i, c):
        pl.semaphore_signal(
            barrier, inc=1, device_id=(lax.rem(e + i, ne), dp), device_id_type=MESH
        )
        return c

    lax.fori_loop(1, ne, greet, 0)
    for to in (side, above, below):
        pl.semaphore_signal(barrier, inc=1, device_id=(e, to), device_id_type=MESH)

    combine = scores[...] / jnp.sum(scores[...], axis=1, keepdims=True)
    slot_e, slot_r = slot[0:1, :], slot[1:2, :]
    tok = tokens.shape[0]
    hit = jnp.zeros((tok, slots), F32)
    weight = jnp.zeros((tok, slots), F32)
    for j in range(routes.shape[1]):
        named = routes[:, j : j + 1] == slot_e
        hit = jnp.where(named, 1.0, hit)
        weight = jnp.where(named, combine[:, j : j + 1], weight)
    rank = dot(lower[...], hit.astype(BF), 1, 0)
    taken = jnp.where(rank == slot_r.astype(F32), hit, 0.0)
    weight = weight * taken
    place[...] = taken.astype(BF)
    high = weight.astype(BF)
    whi[...] = high
    wlo[...] = (weight - high.astype(F32)).astype(BF)

    send_rows = dot(place[...], tokens[...], 0, 0).reshape(ne, CAP, width)
    send_grad = dot(whi[...], ograd[...], 0, 0) + dot(wlo[...], ograd[...], 0, 0)
    both = jnp.concatenate([send_rows, send_grad.reshape(ne, CAP, width)], axis=1)
    disp[...] = both.reshape(ne * BLK, width).astype(BF)
    pl.semaphore_wait(barrier, ne + 2)

    def block(i):
        return pl.ds(pl.multiple_of(i * BLK, BLK), BLK)

    def dispatch(i, c):
        to = lax.rem(e + i, ne)
        far(
            disp.at[block(to)], rbuf.at[0, block(i)], d_send, d_recv.at[i // per], to, dp
        ).start()
        return c

    lax.fori_loop(1, ne, dispatch, 0)
    pltpu.make_async_copy(disp.at[block(e)], rbuf.at[0, block(0)], d_recv.at[0]).start()

    w1 = far(wgu.at[1 - b], wgu2.at[pl.ds(width, width)], w_send.at[0], w_recv.at[0], e, side)
    w2 = far(wd.at[1 - b], wdp, w_send.at[1], w_recv.at[1], e, side)
    w1.start()
    w2.start()
    wgu2[0:width, :] = wgu[b]
    moves = []
    for g in range(GROUPS):
        at = pl.ds(g * per * BLK, per * BLK)
        landed(rbuf.at[0, at], d_recv.at[g])
        move = far(rbuf.at[0, at], rbuf.at[1, at], f_send.at[g], f_recv.at[g], e, side)
        move.start()
        moves.append(move)

    def unpack(which):
        got = rbuf[which].astype(F32).reshape(ne, BLK, width)
        cols = slice(which * width, (which + 1) * width)
        rows[:, cols] = got[:, :CAP].reshape(slots, width).astype(BF)
        grads[:, cols] = got[:, CAP:].reshape(slots, width).astype(BF)

    unpack(0)
    w1.wait_recv()
    w2.wait_recv()
    for move in moves:
        move.wait_recv()
    unpack(1)

    step = slots // 4
    wd2 = jnp.concatenate([wd[b], wdp[...]], axis=1)

    def partial(i, c):
        at = pl.ds(pl.multiple_of(i * step, step), step)
        value = dot(rows[at, :], wgu2[...], 1, 0)
        part[0, at, :] = value[:, :half]
        part[1, at, :] = value[:, half:]
        part[2, at, :] = dot(grads[at, :], wd2, 1, 1)
        return c

    lax.fori_loop(0, 4, partial, 0)

    def of(d):
        return pl.ds(pl.multiple_of(d * share, share), share)

    def sums(up, k, c):
        n = n_up if up else n_dn
        if k < 0 or k >= n:
            return
        d = lax.rem(z + n_up - k, nz) if up else lax.rem(z + nz - n_dn + k, nz)
        send, recv = (ru_send, ru_recv) if up else (rd_send, rd_recv)
        value = part[c, of(d), :]
        if k:
            value = value + arrived(up, k - 1, c)
        if k < narrow:
            src, dst, at = (su_n, ru_n, k) if up else (sd_n, rd_n, k)
        else:
            src, dst, at = (su_w, ru_w, k - narrow) if up else (sd_w, rd_w, k - narrow)
        src[c, at] = value.astype(src.dtype)
        far(
            src.at[c, at], dst.at[c, at], send.at[c, k], recv.at[c, k],
            e, above if up else below,
        ).start()

    def arrived(up, k, c):
        if k < narrow:
            ref, at = (ru_n if up else rd_n), k
        else:
            ref, at = (ru_w if up else rd_w), k - narrow
        landed(ref.at[c, at], (ru_recv if up else rd_recv).at[c, k])
        return ref[c, at].astype(F32)

    def summed(c):
        return part[c, of(z), :] + arrived(False, n_dn - 1, c) + arrived(True, n_up - 1, c)

    def gathers(up, k, c):
        n = n_up if up else n_dn
        if k < 0 or k > n:
            return
        d = lax.rem(z + nz - k, nz) if up else lax.rem(z + k, nz)
        send, recv = (gu_send, gu_recv) if up else (gd_send, gd_recv)
        at = act.at[c, of(d)]
        if k:
            landed(at, recv.at[c, k - 1])
        if k < n:
            far(at, at, send.at[c, k], recv.at[c, k], e, above if up else below).start()

    def finish(d, first):
        hid = act[0, of(d), :]
        both = jnp.concatenate([act[1, of(d), :], act[2, of(d), :]], axis=1)
        eo = dot(hid, jnp.concatenate([wd[b], wdp[...]], axis=1), 1, 0)
        dx = dot(both, wgu2[...], 1, 1)
        own[0, of(d), :] = eo[:, :width]
        own[1, of(d), :] = dx[:, :width]
        xo_s[d] = jnp.concatenate([eo[:, width:], dx[:, width:]], axis=0).astype(BF)
        far(xo_s.at[d], xo_r.at[d], o_send.at[d], o_recv.at[d], e, side).start()
        to_u = dot(rows[of(d), :], both, 0, 0)
        to_d = dot(hid, grads[of(d), :], 0, 0)
        acc_u[...] = to_u if first else acc_u[...] + to_u
        acc_d[...] = to_d if first else acc_d[...] + to_d

    n_blk = share // CAP

    def deliver(d):
        landed(xo_r.at[d], o_recv.at[d])
        got = xo_r[d].astype(F32)
        eo = (own[0, of(d), :] + got[:share]).reshape(n_blk, CAP, width)
        dx = (own[1, of(d), :] + got[share:]).reshape(n_blk, CAP, width)
        whole = jnp.concatenate([eo, dx], axis=1).reshape(n_blk * BLK, width)
        cb_s[pl.ds(pl.multiple_of(d * n_blk * BLK, n_blk * BLK), n_blk * BLK), :] = whole.astype(BF)
        for i in range(n_blk):
            p = d * n_blk + i
            to = lax.rem(e + ne - p, ne)

            @pl.when(p != 0)
            def _():
                far(cb_s.at[block(p)], cb_r.at[block(e)], c_send, c_recv, to, dp).start()

            @pl.when(p == 0)
            def _():
                pltpu.make_async_copy(cb_s.at[block(p)], cb_r.at[block(e)], c_recv).start()

    def at_step(k):
        if k == 0:
            return [z]
        if k > n_dn:
            return [lax.rem(z + nz - k, nz)]
        return [lax.rem(z + nz - k, nz), lax.rem(z + k, nz)]

    for k in range(n_up):
        for c in range(3):
            sums(True, k, c)
            sums(False, k, c)
    gate, upper, grad_hidden = summed(0), summed(1), summed(2)
    sig = jax.nn.sigmoid(gate)
    act[0, of(z), :] = (gate * sig * upper).astype(BF)
    act[1, of(z), :] = (grad_hidden * upper * sig * (1.0 + gate * (1.0 - sig))).astype(BF)
    act[2, of(z), :] = (grad_hidden * (gate * sig)).astype(BF)
    for k in range(n_up + 1):
        for c in range(3):
            gathers(True, k, c)
            gathers(False, k, c)
        for d in at_step(k):
            finish(d, k == 0)
        if k == n_up:
            tg_u[...] = acc_u[width:, :].astype(BF)
            t1 = far(tg_u, ggu.at[b], t_send.at[0], t_recv.at[0], e, side)
            t1.start()
            tg_d[...] = acc_d[:, width:].astype(BF)
            t2 = far(tg_d, gdn.at[b], t_send.at[1], t_recv.at[1], e, side)
            t2.start()
        if k:
            for d in at_step(k - 1):
                deliver(d)
    for d in at_step(n_up):
        deliver(d)
    ggu[b] = acc_u[:width, :].astype(BF)
    gdn[b] = acc_d[:, :width].astype(BF)

    landed(cb_r, c_recv)
    got = cb_r[...].astype(F32).reshape(ne, BLK, width)
    eo = got[:, :CAP].reshape(slots, width).astype(BF)
    dx = got[:, CAP:].reshape(slots, width).astype(BF)
    out[...] = (dot(whi[...], eo, 1, 0) + dot(wlo[...], eo, 1, 0)).astype(BF)
    gtok[...] = dot(place[...], dx, 1, 0).astype(BF)

    t1.wait_recv()
    t2.wait_recv()
    landed(disp.at[pl.ds(0, (ne - 1) * BLK)], d_send)
    landed(cb_s.at[pl.ds(0, (ne - 1) * BLK)], c_send)
    for move in (w1, w2, *moves, t1, t2):
        move.wait_send()
    for d in range(nz):
        landed(xo_s.at[d], o_send.at[d])
    for up, n in ((True, n_up), (False, n_dn)):
        for k in range(n):
            for c in range(3):
                if k < narrow:
                    src, at = (su_n if up else sd_n), k
                else:
                    src, at = (su_w if up else sd_w), k - narrow
                landed(src.at[c, at], (ru_send if up else rd_send).at[c, k])
                landed(act.at[c, pl.ds(0, share)], (gu_send if up else gd_send).at[c, k])


def body(tokens, out_grad, routes, scores, w_gate_up, w_down):
    ne, ndp = lax.axis_size("expert"), lax.axis_size("dp")
    nz = ndp // 2
    tok, width = tokens.shape
    hidden = w_down.shape[1]
    half = hidden // 2
    slots = ne * CAP
    share = slots // nz
    n_up, n_dn = nz // 2, nz // 2 - 1
    narrow = max(1, n_up - WIDE)
    ids = np.arange(slots)
    slot = jnp.asarray(np.stack([ids // CAP, ids % CAP]).astype(np.int32))
    lower = jnp.asarray(np.tril(np.ones((tok, tok), np.float32), -1)).astype(BF)
    wgu = w_gate_up[0].reshape(width, 2, 2, half).transpose(2, 0, 1, 3).reshape(2, width, 2 * half)
    wd = w_down[0].reshape(2, half, width)
    dma = pltpu.SemaphoreType.DMA
    ups = [pltpu.VMEM((3, narrow, share, half), BF)] * 2
    ups += [pltpu.VMEM((3, n_up - narrow, share, half), F32)] * 2
    dns = [pltpu.VMEM((3, narrow, share, half), BF)] * 2
    dns += [pltpu.VMEM((3, max(1, n_dn - narrow), share, half), F32)] * 2
    out, gtok, ggu, gdn = pl.pallas_call(
        functools.partial(kernel, ne, nz),
        out_shape=(
            jax.ShapeDtypeStruct((tok, width), BF),
            jax.ShapeDtypeStruct((tok, width), BF),
            jax.ShapeDtypeStruct((2, width, 2 * half), BF),
            jax.ShapeDtypeStruct((2, half, width), BF),
        ),
        in_specs=[pl.BlockSpec(memory_space=pltpu.VMEM)] * 8,
        out_specs=[pl.BlockSpec(memory_space=pltpu.VMEM)] * 4,
        scratch_shapes=[
            pltpu.VMEM((tok, slots), BF),
            pltpu.VMEM((tok, slots), BF),
            pltpu.VMEM((tok, slots), BF),
            pltpu.VMEM((ne * BLK, width), BF),
            pltpu.VMEM((2, ne * BLK, width), BF),
            pltpu.VMEM((slots, 2 * width), BF),
            pltpu.VMEM((slots, 2 * width), BF),
            pltpu.VMEM((2 * width, 2 * half), BF),
            pltpu.VMEM((half, width), BF),
            pltpu.VMEM((3, slots, half), F32),
            *ups,
            *dns,
            pltpu.VMEM((3, slots, half), BF),
            pltpu.VMEM((nz, 2 * share, width), BF),
            pltpu.VMEM((nz, 2 * share, width), BF),
            pltpu.VMEM((2, slots, width), F32),
            pltpu.VMEM((ne * BLK, width), BF),
            pltpu.VMEM((ne * BLK, width), BF),
            pltpu.VMEM((width, 2 * half), BF),
            pltpu.VMEM((half, width), BF),
            pltpu.VMEM((2 * width, 2 * half), F32),
            pltpu.VMEM((half, 2 * width), F32),
            dma, dma((GROUPS,)),
            dma((2,)), dma((2,)),
            dma((GROUPS,)), dma((GROUPS,)),
            dma((3, n_up)), dma((3, n_up)), dma((3, n_dn)), dma((3, n_dn)),
            dma((3, n_up)), dma((3, n_up)), dma((3, n_dn)), dma((3, n_dn)),
            dma((nz,)), dma((nz,)),
            dma, dma,
            dma((2,)), dma((2,)),
        ],
        compiler_params=pltpu.CompilerParams(
            collective_id=0, has_side_effects=True, vmem_limit_bytes=48 * 1024 * 1024
        ),
    )(routes, scores, tokens, out_grad, wgu, wd, slot, lower)
    grad_first = (
        ggu.reshape(2, width, 2, half).transpose(1, 2, 0, 3).reshape(1, width, 2, hidden)
    )
    return out, gtok, grad_first, gdn.reshape(1, hidden, width)


def solution(mesh):
    placed = (
        P("expert", "dp"),
        P("expert", "dp"),
        P("expert", None),
        P("expert", None),
        P("expert", "dp", None, None),
        P("expert", None, "dp"),
    )
    return jax.shard_map(
        body,
        mesh=mesh,
        in_specs=placed,
        out_specs=(
            P("expert", "dp"),
            P("expert", "dp"),
            P("expert", "dp", None, None),
            P("expert", None, "dp"),
        ),
        check_vma=False,
    )
```

time: 148 us -> 124 us (0.84)
  Pallas kernels: 140 us -> 116 us
    pallas_call x1, Pallas kernels: 140 us -> 116 us  [body(): pl.pallas_call(functools.partial(kernel, ne, nz), out_shape=(jax.ShapeDty...]
where the time goes in v2:
time: 124 us
  Pallas kernels  116 us (94%)
  local copies, waits for them, and re-layouts  7.04 us (6%)
    pallas_call x1, Pallas kernels, body(): pl.pallas_call(functools.partial(kernel, ne, nz), out_shape=(jax.ShapeDty...  116 us
    unnamed x17, local copies, waits for them, and re-layouts  3.54 us

profile of v2, /device:TPU:1, one launch (start us, length us, event | category | flops | bytes accessed | tf_op | source)
XLA Modules:
  0.0 123.6 jit_solution(9970456795235084585)
XLA Ops:
  0.6 0.0 copy-start.5
  0.6 0.8 copy.13.routes
  1.5 0.0 copy-done.5
  1.5 0.1 copy.14.scores
  1.6 1.3 %reshape_squeeze.6 = bf16[128,2,2,384]{3,2,1,0:T(2,128)(2,1)S(1)} reshape(bf16[1,128,2,768]{3,2,1,0:T(2,128)(2,1)} %param.12) | data formatting | bytes 786432 | tf_op jit(solution)/shard_map/reshape;squeeze | solution.py:302
  2.8 0.3 copy.17
  3.1 0.0 copy-start
  3.2 0.0 copy-start.1
  3.2 0.0 copy-start.2
  3.2 0.0 copy-start.3
  3.2 0.0 copy-start.4
  3.2 0.2 reshape.20.wgu
  3.5 0.6 copy-done
  4.1 0.1 copy-done.1
  4.1 0.0 copy-done.2
  4.1 0.0 copy-done.3
  4.1 0.0 copy-done.4
  4.1 115.8 %shard_map.111 = (bf16[192,128]{1,0:T(8,128)(2,1)S(1)}, bf16[192,128]{1,0:T(8,128)(2,1)S(1)}, bf16[2,128,768]{2,1,0:T(8,128)(2,1)S(1)}, bf16[2,384,128]{2,1,0:T(8,128)(2,1)S(1)}) custom-call(s32[192,8]{1,0:T(8,128)S(1)} %copy.13.routes, f32[192,8]{1,0:T(8,128)S(1)} %copy.14.scores, bf16[192,128]{1,0:T(8,128)(2,1)S(1)} %copy-done.2, ...), custom_call_target="tpu_custom_call" | custom-call | tf_op jit(solution)/shard_map/pallas_call | solution.py:309
  120.0 0.1 reshape.21
  120.1 0.6 copy.15
  120.7 1.0 reshape.22
  121.7 0.6 copy.21
  122.3 0.6 copy.22
  122.9 0.7 copy.23
Async XLA Ops:
  0.6 0.8 copy-start.5
  3.1 0.9 copy-start
  3.2 1.0 copy-start.1
  3.2 1.0 copy-start.2
  3.2 1.0 copy-start.3
  3.2 1.0 copy-start.4

commit v3 on v2

--- a/solution.py
+++ b/solution.py
@@ -11,7 +11,7 @@
 CAP = 24
 BLK = 2 * CAP
 GROUPS = 8
-WIDE = 2
+WIDE = 3
 MESH = pl.DeviceIdType.MESH
 BF = jnp.bfloat16
 F32 = jnp.float32
@@ -49,6 +49,15 @@
     n_up, n_dn = nz // 2, nz // 2 - 1
     narrow = max(1, n_up - WIDE)
     per = ne // GROUPS
+    mid = ne // 2
+
+    def partner(i):
+        to = lax.rem(e // mid + i // mid, 2) * mid + lax.rem(e + i, mid)
+        return to, lax.rem(b + i // mid, 2) * nz + z
+
+    def sender(i):
+        to = lax.rem(e // mid + i // mid, 2) * mid + lax.rem(e + ne - i, mid)
+        return to, lax.rem(b + i // mid, 2) * nz + z
 
     def far(src, dst, send, recv, to_e, to_dp):
         return pltpu.make_async_remote_copy(
@@ -59,9 +68,7 @@
     barrier = pltpu.get_barrier_semaphore()
 
     def greet(i, c):
-        pl.semaphore_signal(
-            barrier, inc=1, device_id=(lax.rem(e + i, ne), dp), device_id_type=MESH
-        )
+        pl.semaphore_signal(barrier, inc=1, device_id=partner(i), device_id_type=MESH)
         return c
 
     lax.fori_loop(1, ne, greet, 0)
@@ -95,9 +102,9 @@
         return pl.ds(pl.multiple_of(i * BLK, BLK), BLK)
 
     def dispatch(i, c):
-        to = lax.rem(e + i, ne)
+        to, col = partner(i)
         far(
-            disp.at[block(to)], rbuf.at[0, block(i)], d_send, d_recv.at[i // per], to, dp
+            disp.at[block(to)], rbuf.at[i // mid, block(i)], d_send, d_recv.at[i // per], to, col
         ).start()
         return c
 
@@ -112,8 +119,10 @@
     moves = []
     for g in range(GROUPS):
         at = pl.ds(g * per * BLK, per * BLK)
-        landed(rbuf.at[0, at], d_recv.at[g])
-        move = far(rbuf.at[0, at], rbuf.at[1, at], f_send.at[g], f_recv.at[g], e, side)
+        part_of = g * per // mid
+        here, there = rbuf.at[part_of, at], rbuf.at[1 - part_of, at]
+        landed(here, d_recv.at[g])
+        move = far(here, there, f_send.at[g], f_recv.at[g], e, side)
         move.start()
         moves.append(move)
 
@@ -123,11 +132,11 @@
         rows[:, cols] = got[:, :CAP].reshape(slots, width).astype(BF)
         grads[:, cols] = got[:, CAP:].reshape(slots, width).astype(BF)
 
-    unpack(0)
     w1.wait_recv()
     w2.wait_recv()
     for move in moves:
         move.wait_recv()
+    unpack(0)
     unpack(1)
 
     step = slots // 4
@@ -193,9 +202,19 @@
         both = jnp.concatenate([act[1, of(d), :], act[2, of(d), :]], axis=1)
         eo = dot(hid, jnp.concatenate([wd[b], wdp[...]], axis=1), 1, 0)
         dx = dot(both, wgu2[...], 1, 1)
-        own[0, of(d), :] = eo[:, :width]
-        own[1, of(d), :] = dx[:, :width]
-        xo_s[d] = jnp.concatenate([eo[:, width:], dx[:, width:]], axis=0).astype(BF)
+        mine = jnp.concatenate([eo[:, :width], dx[:, :width]], axis=0)
+        other = jnp.concatenate([eo[:, width:], dx[:, width:]], axis=0)
+
+        @pl.when(d < nz // 2)
+        def _():
+            own[d] = mine
+            xo_s[d] = other.astype(BF)
+
+        @pl.when(d >= nz // 2)
+        def _():
+            own[d] = other
+            xo_s[d] = mine.astype(BF)
+
         far(xo_s.at[d], xo_r.at[d], o_send.at[d], o_recv.at[d], e, side).start()
         to_u = dot(rows[of(d), :], both, 0, 0)
         to_d = dot(hid, grads[of(d), :], 0, 0)
@@ -206,18 +225,18 @@
 
     def deliver(d):
         landed(xo_r.at[d], o_recv.at[d])
-        got = xo_r[d].astype(F32)
-        eo = (own[0, of(d), :] + got[:share]).reshape(n_blk, CAP, width)
-        dx = (own[1, of(d), :] + got[share:]).reshape(n_blk, CAP, width)
+        got = own[d] + xo_r[d].astype(F32)
+        eo = got[:share].reshape(n_blk, CAP, width)
+        dx = got[share:].reshape(n_blk, CAP, width)
         whole = jnp.concatenate([eo, dx], axis=1).reshape(n_blk * BLK, width)
         cb_s[pl.ds(pl.multiple_of(d * n_blk * BLK, n_blk * BLK), n_blk * BLK), :] = whole.astype(BF)
         for i in range(n_blk):
             p = d * n_blk + i
-            to = lax.rem(e + ne - p, ne)
+            to, col = sender(p)
 
             @pl.when(p != 0)
             def _():
-                far(cb_s.at[block(p)], cb_r.at[block(e)], c_send, c_recv, to, dp).start()
+                far(cb_s.at[block(p)], cb_r.at[block(e)], c_send, c_recv, to, col).start()
 
             @pl.when(p == 0)
             def _():
@@ -332,7 +351,7 @@
             pltpu.VMEM((3, slots, half), BF),
             pltpu.VMEM((nz, 2 * share, width), BF),
             pltpu.VMEM((nz, 2 * share, width), BF),
-            pltpu.VMEM((2, slots, width), F32),
+            pltpu.VMEM((nz, 2 * share, width), F32),
             pltpu.VMEM((ne * BLK, width), BF),
             pltpu.VMEM((ne * BLK, width), BF),
             pltpu.VMEM((width, 2 * half), BF),

time: 124 us -> 120 us (0.968)
  Pallas kernels: 116 us -> 112 us
    pallas_call x1, Pallas kernels: 116 us -> 112 us  [body(): pl.pallas_call(functools.partial(kernel, ne, nz), out_shape=(jax.ShapeDty...]
where the time goes in v3:
time: 120 us
  Pallas kernels  112 us (93%)
  local copies, waits for them, and re-layouts  7.04 us (6%)
    pallas_call x1, Pallas kernels, body(): pl.pallas_call(functools.partial(kernel, ne, nz), out_shape=(jax.ShapeDty...  112 us
    unnamed x17, local copies, waits for them, and re-layouts  3.54 us

profile of v3, /device:TPU:1, one launch (start us, length us, event | category | flops | bytes accessed | tf_op | source)
XLA Modules:
  0.0 119.8 jit_solution(237668173094953771)
XLA Ops:
  0.6 0.0 copy-start.5
  0.6 0.8 copy.13.routes
  1.5 0.0 copy-done.5
  1.5 0.1 copy.14.scores
  1.6 1.3 %reshape_squeeze.6 = bf16[128,2,2,384]{3,2,1,0:T(2,128)(2,1)S(1)} reshape(bf16[1,128,2,768]{3,2,1,0:T(2,128)(2,1)} %param.12) | data formatting | bytes 786432 | tf_op jit(solution)/shard_map/reshape;squeeze | solution.py:321
  2.8 0.3 copy.17
  3.1 0.0 copy-start
  3.2 0.0 copy-start.1
  3.2 0.0 copy-start.2
  3.2 0.0 copy-start.3
  3.2 0.0 copy-start.4
  3.2 0.2 reshape.20.wgu
  3.5 0.6 copy-done
  4.1 0.1 copy-done.1
  4.1 0.0 copy-done.2
  4.1 0.0 copy-done.3
  4.1 0.0 copy-done.4
  4.1 112.0 %shard_map.111 = (bf16[192,128]{1,0:T(8,128)(2,1)S(1)}, bf16[192,128]{1,0:T(8,128)(2,1)S(1)}, bf16[2,128,768]{2,1,0:T(8,128)(2,1)S(1)}, bf16[2,384,128]{2,1,0:T(8,128)(2,1)S(1)}) custom-call(s32[192,8]{1,0:T(8,128)S(1)} %copy.13.routes, f32[192,8]{1,0:T(8,128)S(1)} %copy.14.scores, bf16[192,128]{1,0:T(8,128)(2,1)S(1)} %copy-done.2, ...), custom_call_target="tpu_custom_call" | custom-call | tf_op jit(solution)/shard_map/pallas_call | solution.py:328
  116.2 0.1 reshape.21
  116.3 0.6 copy.15
  116.9 1.0 reshape.22
  117.9 0.6 copy.21
  118.5 0.6 copy.22
  119.1 0.7 copy.23
Async XLA Ops:
  0.6 0.8 copy-start.5
  3.1 0.9 copy-start
  3.2 1.0 copy-start.1
  3.2 1.0 copy-start.2
  3.2 1.0 copy-start.3
  3.2 1.0 copy-start.4

commit v4 on v3

--- a/solution.py
+++ b/solution.py
@@ -75,6 +75,12 @@
     for to in (side, above, below):
         pl.semaphore_signal(barrier, inc=1, device_id=(e, to), device_id_type=MESH)
 
+    pl.semaphore_wait(barrier, ne + 2)
+    w1 = far(wgu.at[1 - b], wgu2.at[pl.ds(width, width)], w_send.at[0], w_recv.at[0], e, side)
+    w2 = far(wd.at[1 - b], wdp, w_send.at[1], w_recv.at[1], e, side)
+    w1.start()
+    w2.start()
+
     combine = scores[...] / jnp.sum(scores[...], axis=1, keepdims=True)
     slot_e, slot_r = slot[0:1, :], slot[1:2, :]
     tok = tokens.shape[0]
@@ -96,7 +102,6 @@
     send_grad = dot(whi[...], ograd[...], 0, 0) + dot(wlo[...], ograd[...], 0, 0)
     both = jnp.concatenate([send_rows, send_grad.reshape(ne, CAP, width)], axis=1)
     disp[...] = both.reshape(ne * BLK, width).astype(BF)
-    pl.semaphore_wait(barrier, ne + 2)
 
     def block(i):
         return pl.ds(pl.multiple_of(i * BLK, BLK), BLK)
@@ -111,10 +116,6 @@
     lax.fori_loop(1, ne, dispatch, 0)
     pltpu.make_async_copy(disp.at[block(e)], rbuf.at[0, block(0)], d_recv.at[0]).start()
 
-    w1 = far(wgu.at[1 - b], wgu2.at[pl.ds(width, width)], w_send.at[0], w_recv.at[0], e, side)
-    w2 = far(wd.at[1 - b], wdp, w_send.at[1], w_recv.at[1], e, side)
-    w1.start()
-    w2.start()
     wgu2[0:width, :] = wgu[b]
     moves = []
     for g in range(GROUPS):
@@ -126,18 +127,24 @@
         move.start()
         moves.append(move)
 
-    def unpack(which):
-        got = rbuf[which].astype(F32).reshape(ne, BLK, width)
+    def unpack(which, upper):
+        at = pl.ds(upper * mid * BLK, mid * BLK)
+        to = pl.ds(upper * mid * CAP, mid * CAP)
+        got = rbuf[which, at, :].astype(F32).reshape(mid, BLK, width)
         cols = slice(which * width, (which + 1) * width)
-        rows[:, cols] = got[:, :CAP].reshape(slots, width).astype(BF)
-        grads[:, cols] = got[:, CAP:].reshape(slots, width).astype(BF)
-
+        rows[to, cols] = got[:, :CAP].reshape(mid * CAP, width).astype(BF)
+        grads[to, cols] = got[:, CAP:].reshape(mid * CAP, width).astype(BF)
+
+    unpack(0, 0)
+    unpack(1, 1)
     w1.wait_recv()
     w2.wait_recv()
-    for move in moves:
+    for move in moves[: GROUPS // 2]:
         move.wait_recv()
-    unpack(0)
-    unpack(1)
+    unpack(1, 0)
+    for move in moves[GROUPS // 2 :]:
+        move.wait_recv()
+    unpack(0, 1)
 
     step = slots // 4
     wd2 = jnp.concatenate([wd[b], wdp[...]], axis=1)

time: 120 us -> 122 us (1.017)
  Pallas kernels: 112 us -> 114 us
    pallas_call x1, Pallas kernels: 112 us -> 114 us  [body(): pl.pallas_call(functools.partial(kernel, ne, nz), out_shape=(jax.ShapeDty...]
where the time goes in v4:
time: 122 us; the launch traced here: 121 us
  Pallas kernels  114 us (93%)
  local copies, waits for them, and re-layouts  7.04 us (6%)
    pallas_call x1, Pallas kernels, body(): pl.pallas_call(functools.partial(kernel, ne, nz), out_shape=(jax.ShapeDty...  114 us
    unnamed x17, local copies, waits for them, and re-layouts  3.54 us

profile of v4, /device:TPU:1, one launch (start us, length us, event | category | flops | bytes accessed | tf_op | source)
XLA Modules:
  0.0 121.4 jit_solution(8190904530998936334)
XLA Ops:
  0.6 0.0 copy-start.5
  0.6 0.8 copy.13.routes
  1.5 0.0 copy-done.5
  1.5 0.1 copy.14.scores
  1.6 1.3 %reshape_squeeze.6 = bf16[128,2,2,384]{3,2,1,0:T(2,128)(2,1)S(1)} reshape(bf16[1,128,2,768]{3,2,1,0:T(2,128)(2,1)} %param.12) | data formatting | bytes 786432 | tf_op jit(solution)/shard_map/reshape;squeeze | solution.py:328
  2.8 0.3 copy.17
  3.1 0.0 copy-start
  3.2 0.0 copy-start.1
  3.2 0.0 copy-start.2
  3.2 0.0 copy-start.3
  3.2 0.0 copy-start.4
  3.2 0.2 reshape.20.wgu
  3.5 0.6 copy-done
  4.1 0.1 copy-done.1
  4.1 0.0 copy-done.2
  4.1 0.0 copy-done.3
  4.1 0.0 copy-done.4
  4.1 113.6 %shard_map.111 = (bf16[192,128]{1,0:T(8,128)(2,1)S(1)}, bf16[192,128]{1,0:T(8,128)(2,1)S(1)}, bf16[2,128,768]{2,1,0:T(8,128)(2,1)S(1)}, bf16[2,384,128]{2,1,0:T(8,128)(2,1)S(1)}) custom-call(s32[192,8]{1,0:T(8,128)S(1)} %copy.13.routes, f32[192,8]{1,0:T(8,128)S(1)} %copy.14.scores, bf16[192,128]{1,0:T(8,128)(2,1)S(1)} %copy-done.2, ...), custom_call_target="tpu_custom_call" | custom-call | tf_op jit(solution)/shard_map/pallas_call | solution.py:335
  117.8 0.1 reshape.21
  117.9 0.6 copy.15
  118.5 1.0 reshape.22
  119.5 0.6 copy.21
  120.1 0.6 copy.22
  120.7 0.7 copy.23
Async XLA Ops:
  0.6 0.8 copy-start.5
  3.1 0.9 copy-start
  3.2 1.0 copy-start.1
  3.2 1.0 copy-start.2
  3.2 1.0 copy-start.3
  3.2 1.0 copy-start.4
